TPU v7x, 32 devices: a whole 2x2x4 slice. The times are simulated.
32 devices in a mesh: grp: 2 (over y), row: 8 (over z, x), ch: 1, sub: 2 (over core).
Axes of the slice: x: 2, y: 2, z: 4, core: 2. Of those that a mesh axis runs over, the one named last changes fastest.
Arguments:
- pair_field: bfloat16 [128, 256, 128], P(None, ('grp', 'row', 'sub'), 'ch'), parts along dimension 1, may hold values from -6 to 6
- residue_mask: int32 [256], P('grp'), parts along dimension 0, may hold values from 0 to 1, as said below
- input_gain: float32 [2, 128], replicated, may hold values from 0.1 to 1.9
- projection_weight: bfloat16 [2, 128, 512], replicated, may hold values from -0.5 to 0.5
- gate_weight: bfloat16 [2, 128, 128], replicated, may hold values from -0.5 to 0.5
- output_gain: float32 [2, 128], replicated, may hold values from 0.1 to 1.9
- output_weight: bfloat16 [2, 128, 128], replicated, may hold values from -0.5 to 0.5
Outputs:
- updated_pair: bfloat16 [128, 256, 128], P(None, ('grp', 'row', 'sub'), 'ch'), parts along dimension 1
There are 2 independent parts, one for each index of `grp`. A program takes and returns all parts, laid end to end along the dimension named above; an argument that names none is the same for every part. Nothing has to cross between parts.
Inputs may be any that keep to these rules, and one draw needn't show every extreme that they name: `residue_mask`: ones at positions 0 up to some count and zeros after it; at least 64 ones and at least one zero.
All inputs are finite; a program needn't handle non-finite values.
Results may differ from a plain program's by a relative error of at most 0.015.
Values may be sent and summed in bfloat16 or wider, within the bound.
A program may use at most 64 MiB of HBM per device.

v0:
```python
import jax
import jax.numpy as jnp
from jax import lax
from jax.sharding import PartitionSpec as P

EPS = 1e-05


def channel_norm(values, gain_vector):
    average = jnp.mean(values, axis=0, keepdims=True)
    centred = values - average
    spread = jnp.mean(centred * centred, axis=0, keepdims=True)
    return centred * lax.rsqrt(spread + EPS) * gain_vector[:, None, None]


def body(
    pair_field, residue_mask, input_gain, projection_weight, gate_weight, output_gain, output_weight
):
    rows_count = lax.axis_size("row")
    chan_count = lax.axis_size("ch")
    halves = lax.axis_size("sub")
    local_rows = pair_field.shape[1]
    local_cols = pair_field.shape[2]
    length = residue_mask.shape[0]
    hidden = output_weight.shape[1]
    per_device = hidden // (rows_count * chan_count)
    used_rows = length // halves
    half_index = lax.axis_index("sub")
    mask_float = residue_mask.astype(jnp.float32)
    row_mask = lax.dynamic_slice_in_dim(
        mask_float, (lax.axis_index("row") * halves + half_index) * local_rows, local_rows
    )
    col_mask = lax.dynamic_slice_in_dim(mask_float, lax.axis_index("ch") * local_cols, local_cols)
    pair_mask = row_mask[:, None] * col_mask[None, :]

    def arrange_rows(values):
        shaped = values.reshape(per_device, rows_count, chan_count, local_rows, local_cols)
        return shaped.transpose(0, 1, 3, 2, 4).reshape(per_device, used_rows, length)

    current = pair_field
    for update in range(2):
        normed = channel_norm(current.astype(jnp.float32), input_gain[update]).astype(jnp.bfloat16)
        projected = jnp.einsum(
            "dpq,de->epq", normed, projection_weight[update], preferred_element_type=jnp.float32
        )
        gate_value = jax.nn.sigmoid(
            jnp.einsum(
                "dpq,de->epq", normed, gate_weight[update], preferred_element_type=jnp.float32
            )
        )
        left_proj = (
            pair_mask * jax.nn.sigmoid(projected[hidden : 2 * hidden]) * projected[:hidden]
        ).astype(jnp.bfloat16)
        right_proj = (
            pair_mask * jax.nn.sigmoid(projected[3 * hidden :]) * projected[2 * hidden : 3 * hidden]
        ).astype(jnp.bfloat16)
        moved_left = lax.all_to_all(
            left_proj.reshape(hidden, 1, local_rows, local_cols),
            ("row", "ch"),
            split_axis=0,
            concat_axis=1,
            tiled=True,
        )
        moved_right = lax.all_to_all(
            right_proj.reshape(hidden, 1, local_rows, local_cols),
            ("row", "ch"),
            split_axis=0,
            concat_axis=1,
            tiled=True,
        )
        left_chan = arrange_rows(moved_left)
        right_chan = arrange_rows(moved_right)
        if update == 0:
            stacked = right_chan.reshape(per_device, rows_count, 1, local_rows, length)
            result = jnp.einsum(
                "cik,crptk->cirpt",
                left_chan,
                lax.all_gather(stacked, "sub", axis=2, tiled=True),
                preferred_element_type=jnp.float32,
            )
            mixed_hidden = result.reshape(per_device, used_rows, length).astype(jnp.bfloat16)
        else:
            left_stack = left_chan.reshape(per_device, rows_count, 1, local_rows, length)
            right_stack = right_chan.reshape(per_device, rows_count, 1, local_rows, length)
            shard_left = lax.all_gather(left_stack, "sub", axis=2, tiled=True)
            shard_right = lax.all_gather(right_stack, "sub", axis=2, tiled=True)
            span_count = shard_left.shape[2]
            accumulate_shaped = shard_left.reshape(
                per_device, rows_count, span_count, local_rows, rows_count, halves, local_rows
            )
            chosen = lax.dynamic_slice_in_dim(accumulate_shaped, half_index, 1, 5)
            chosen = chosen.reshape(per_device, rows_count, span_count, local_rows, used_rows)
            total = jnp.einsum(
                "crpti,crptj->cij", chosen, shard_right, preferred_element_type=jnp.float32
            )
            mixed_hidden = total.astype(jnp.bfloat16)
        from_shaped = mixed_hidden.reshape(
            per_device, rows_count, local_rows, chan_count, local_cols
        )
        arranged = from_shaped.transpose(0, 1, 3, 2, 4).reshape(
            per_device, rows_count * chan_count, local_rows, local_cols
        )
        returned = lax.all_to_all(arranged, ("row", "ch"), split_axis=1, concat_axis=0, tiled=True)
        mixed_rows = returned.reshape(hidden, local_rows, local_cols)
        gain_vector = output_gain[update]
        weight_rows = output_weight[update]
        mixed_norm = channel_norm(mixed_rows.astype(jnp.float32), gain_vector).astype(jnp.bfloat16)
        update_term = jnp.einsum(
            "dpq,de->epq", mixed_norm, weight_rows, preferred_element_type=jnp.float32
        )
        current = (current.astype(jnp.float32) + gate_value * update_term).astype(jnp.bfloat16)
    return current


def solution(mesh):
    placed = (P(None, ("grp", "row", "sub"), "ch"), P("grp"), P(), P(), P(), P(), P())
    return jax.shard_map(
        body,
        mesh=mesh,
        in_specs=placed,
        out_specs=P(None, ("grp", "row", "sub"), "ch"),
        check_vma=False,
    )
```

profile of v0, /device:TPU:0, one launch (start us, length us, event | category | flops | bytes accessed | tf_op | source)
XLA Modules:
  0.0 99.0 jit_solution(5770343989547988907)
XLA Ops:
  0.0 0.7 convert_element_type.83
  0.7 0.1 dynamic_slice.7
  0.7 0.1 broadcast_multiply_fusion
  0.8 1.0 convert_reduce_fusion
  1.8 1.0 %fusion.17 = f32[8,128]{1,0:T(8,128)S(1)} fusion(f32[8,128]{1,0:T(8,128)S(1)} %broadcast_multiply_fusion.4, bf16[128,8,128]{2,1,0:T(8,128)(2,1)} %param.7), kind=kLoop, calls=%fused_computation.28 | loop fusion | flops 523264 | bytes 270336 | tf_op jit(solution)/shard_map/reduce_sum | solution.py:12
  2.8 0.8 slice_bitcast_fusion
  3.6 1.5 %convolution_bitcast_fusion.1 = f32[512,8,128]{0,2,1:T(8,128)S(1)} fusion(bf16[2,128,512]{2,1,0:T(8,128)(2,1)} %param.10, f32[128]{0:T(128)S(1)} %get-tuple-element.12, f32[8,128]{1,0:T(8,128)S(1)} %add_rsqrt_fusion.3, f32[8,128]{1,0:T(8,128)S(1)} %broadcast_multiply_fusion.4, bf16[128,8,128]{2,1,0:T(8,128)(2,1)} %param.7), kind=kOutput, calls=%fused_computation.2 | convolution fusion | flops 134873088 | bytes 2499072 | tf_op jit(solution)/shard_map/dpq,de->epq/dot_general | solution.py:43
  5.1 0.3 fusion.58
  5.4 0.9 copy.76
  6.3 7.3 %all-to-all-start.1 = ((bf16[128,1,8,128]{3,2,1,0:T(8,128)(2,1)}), bf16[128,1,8,128]{3,2,1,0:T(8,128)(2,1)S(1)}, u32[]{:S(2)}, u32[]{:S(2)}) async-start(bf16[128,1,8,128]{3,2,1,0:T(8,128)(2,1)} %copy.76), calls=%async_computation.1 | async-start | bytes 524288 | tf_op jit(solution)/shard_map/all_to_all | solution.py:64
  13.6 0.9 copy.74
  14.4 8.0 %all-to-all-done.1 = bf16[128,1,8,128]{3,2,1,0:T(8,128)(2,1)S(1)} async-done(((bf16[128,1,8,128]{3,2,1,0:T(8,128)(2,1)}), bf16[128,1,8,128]{3,2,1,0:T(8,128)(2,1)S(1)}, u32[]{:S(2)}, u32[]{:S(2)}) %all-to-all-start.1) | async-done | bytes 262176 | tf_op jit(solution)/shard_map/all_to_all | solution.py:64
  22.5 3.6 %all-to-all-start = ((bf16[128,1,8,128]{3,2,1,0:T(8,128)(2,1)}), bf16[128,1,8,128]{3,2,1,0:T(8,128)(2,1)S(1)}, u32[]{:S(2)}, u32[]{:S(2)}) async-start(bf16[128,1,8,128]{3,2,1,0:T(8,128)(2,1)} %copy.74), calls=%async_computation | async-start | bytes 524288 | tf_op jit(solution)/shard_map/all_to_all | solution.py:57
  26.1 0.1 copy.123
  26.1 2.2 %all_gather.9 = bf16[16,8,2,8,128]{4,3,2,1,0:T(8,128)(2,1)S(1)} all-gather(bf16[16,8,1,8,128]{4,3,2,1,0:T(8,128)(2,1)S(1)} %bitcast.145), channel_id=1, replica_groups=mesh['grp'=2,'row'=8,'ch'=1,'sub'=2] {'sub'}, dimensions={2}, use_global_device_ids=true | all-gather | bytes 786432 | tf_op jit(solution)/shard_map/all_gather | solution.py:78
  28.3 6.3 %all-to-all-done = bf16[128,1,8,128]{3,2,1,0:T(8,128)(2,1)S(1)} async-done(((bf16[128,1,8,128]{3,2,1,0:T(8,128)(2,1)}), bf16[128,1,8,128]{3,2,1,0:T(8,128)(2,1)S(1)}, u32[]{:S(2)}, u32[]{:S(2)}) %all-to-all-start) | async-done | bytes 262176 | tf_op jit(solution)/shard_map/all_to_all | solution.py:57
  34.6 0.3 convolution_convert_fusion
  34.9 3.4 %copy.78 = bf16[16,64,8,2,8]{0,4,3,2,1:T(8,128)(2,1)S(1)} copy(bf16[16,64,8,2,8]{1,4,3,2,0:T(8,128)(2,1)S(1)} %convolution_convert_fusion) | data formatting | bytes 524288 | tf_op jit(solution)/shard_map/convert_element_type | solution.py:81
  38.3 0.0 copy-start.3
  38.3 0.0 copy-start
  38.3 0.0 copy-start.4
  38.4 1.5 %copy.79 = bf16[16,8,8,128]{3,2,0,1:T(8,128)(2,1)} copy(bf16[16,8,8,128]{0,3,2,1:T(8,128)(2,1)S(1)} %bitcast.141) | data formatting | bytes 524288 | tf_op jit(solution)/shard_map/convert_element_type | solution.py:81
  39.8 0.0 copy-start.2
  39.8 3.7 %all-to-all-start.2 = ((bf16[16,8,8,128]{3,2,0,1:T(8,128)(2,1)}), bf16[16,8,8,128]{3,2,0,1:T(8,128)(2,1)S(1)}, u32[]{:S(2)}, u32[]{:S(2)}) async-start(bf16[16,8,8,128]{3,2,0,1:T(8,128)(2,1)} %copy.79), calls=%async_computation.2 | async-start | bytes 524288 | tf_op jit(solution)/shard_map/all_to_all | solution.py:103
  43.6 0.0 copy-done.3
  43.6 0.1 mul.177
  43.7 0.0 copy-done
  43.7 0.0 copy-done.4
  43.7 0.4 fusion.3
  44.0 0.0 copy-start.1
  44.1 8.0 %all-to-all-done.2 = bf16[16,8,8,128]{3,2,0,1:T(8,128)(2,1)S(1)} async-done(((bf16[16,8,8,128]{3,2,0,1:T(8,128)(2,1)}), bf16[16,8,8,128]{3,2,0,1:T(8,128)(2,1)S(1)}, u32[]{:S(2)}, u32[]{:S(2)}) %all-to-all-start.2) | async-done | bytes 262176 | tf_op jit(solution)/shard_map/all_to_all | solution.py:103
  52.1 0.1 fusion.48
  52.2 0.1 fusion.51
  52.4 0.2 fusion.53
  52.6 0.0 copy-done.2
  52.6 0.3 fusion.76
  52.9 0.1 multiply_reduce_fusion
  53.0 0.0 copy-done.1
  53.0 0.5 convolution_bitcast_fusion
  53.5 0.3 fusion.61
  53.8 0.9 copy.85
  54.7 3.5 %all-to-all-start.3 = ((bf16[128,1,8,128]{3,2,1,0:T(8,128)(2,1)}), bf16[128,1,8,128]{3,2,1,0:T(8,128)(2,1)S(1)}, u32[]{:S(2)}, u32[]{:S(2)}) async-start(bf16[128,1,8,128]{3,2,1,0:T(8,128)(2,1)} %copy.85), calls=%async_computation.3 | async-start | bytes 524288 | tf_op jit(solution)/shard_map/all_to_all | solution.py:57
  58.2 0.9 copy.88
  59.1 7.7 %all-to-all-done.3 = bf16[128,1,8,128]{3,2,1,0:T(8,128)(2,1)S(1)} async-done(((bf16[128,1,8,128]{3,2,1,0:T(8,128)(2,1)}), bf16[128,1,8,128]{3,2,1,0:T(8,128)(2,1)S(1)}, u32[]{:S(2)}, u32[]{:S(2)}) %all-to-all-start.3) | async-done | bytes 262176 | tf_op jit(solution)/shard_map/all_to_all | solution.py:57
  66.7 3.5 %all-to-all-start.4 = ((bf16[128,1,8,128]{3,2,1,0:T(8,128)(2,1)}), bf16[128,1,8,128]{3,2,1,0:T(8,128)(2,1)S(1)}, u32[]{:S(2)}, u32[]{:S(2)}) async-start(bf16[128,1,8,128]{3,2,1,0:T(8,128)(2,1)} %copy.88), calls=%async_computation.4 | async-start | bytes 524288 | tf_op jit(solution)/shard_map/all_to_all | solution.py:64
  70.2 0.1 copy.86
  70.3 2.2 %all_gather.10 = bf16[16,8,2,8,128]{4,3,1,0,2:T(8,128)(2,1)S(1)} all-gather(bf16[16,8,1,8,128]{4,3,1,0,2:T(8,128)(2,1)S(1)} %copy.86), channel_id=1, replica_groups=mesh['grp'=2,'row'=8,'ch'=1,'sub'=2] {'sub'}, dimensions={2}, use_global_device_ids=true | all-gather | bytes 786432 | tf_op jit(solution)/shard_map/all_gather | solution.py:85
  72.5 3.2 %copy.87 = bf16[16,8,2,8,128]{0,4,3,2,1:T(8,128)(2,1)} copy(bf16[16,8,2,8,128]{4,3,1,0,2:T(8,128)(2,1)S(1)} %all_gather.10) | data formatting | bytes 1048576 | tf_op jit(solution)/shard_map/all_gather | solution.py:85
  75.7 1.8 %dynamic-slice_bitcast_fusion = bf16[16,8,2,8,64]{0,4,3,2,1:T(8,128)(2,1)S(1)} fusion(bf16[16,8,2,8,8,2,8]{0,6,5,4,3,2,1:T(8,128)(2,1)} %bitcast.140, s32[]{:T(128)S(6)} %select_n.8), kind=kLoop, calls=%fused_computation | loop fusion | bytes 524292 | tf_op jit(solution)/shard_map/reshape | solution.py:92
  77.5 1.3 %copy.90 = bf16[16,8,2,8,64]{4,3,1,2,0:T(8,128)(2,1)S(1)} copy(bf16[16,8,2,8,64]{0,4,3,2,1:T(8,128)(2,1)S(1)} %dynamic-slice_bitcast_fusion) | data formatting | bytes 524288 | tf_op jit(solution)/shard_map/reshape | solution.py:92
  78.8 0.0 all-to-all-done.4
  78.8 0.1 copy.122
  78.9 2.2 %all_gather.11 = bf16[16,8,2,8,128]{4,3,1,2,0:T(8,128)(2,1)S(1)} all-gather(bf16[16,8,1,8,128]{4,3,1,2,0:T(8,128)(2,1)S(1)} %bitcast.146), channel_id=1, replica_groups=mesh['grp'=2,'row'=8,'ch'=1,'sub'=2] {'sub'}, dimensions={2}, use_global_device_ids=true | all-gather | bytes 786432 | tf_op jit(solution)/shard_map/all_gather | solution.py:86
  81.1 0.3 fusion.14
  81.4 0.8 copy.91
  82.1 6.0 %all-to-all-start.5 = ((bf16[16,8,8,128]{3,2,0,1:T(8,128)(2,1)}), bf16[16,8,8,128]{3,2,0,1:T(8,128)(2,1)S(1)}, u32[]{:S(2)}, u32[]{:S(2)}) async-start(bf16[16,8,8,128]{3,2,0,1:T(8,128)(2,1)} %copy.91), calls=%async_computation.5 | async-start | bytes 524288 | tf_op jit(solution)/shard_map/all_to_all | solution.py:103
  88.1 0.1 mul.194
  88.2 0.4 fusion.7
  88.6 8.8 %all-to-all-done.5 = bf16[16,8,8,128]{3,2,0,1:T(8,128)(2,1)S(1)} async-done(((bf16[16,8,8,128]{3,2,0,1:T(8,128)(2,1)}), bf16[16,8,8,128]{3,2,0,1:T(8,128)(2,1)S(1)}, u32[]{:S(2)}, u32[]{:S(2)}) %all-to-all-start.5) | async-done | bytes 262176 | tf_op jit(solution)/shard_map/all_to_all | solution.py:103
  97.4 0.1 fusion.41
  97.5 0.1 fusion.44
  97.7 0.2 fusion.46
  97.9 0.3 fusion.12
  98.1 0.9 copy.94
  (9 shorter events, 0.1 us)
Async XLA Ops:
  6.3 16.2 %all-to-all-start.1 = ((bf16[128,1,8,128]{3,2,1,0:T(8,128)(2,1)}), bf16[128,1,8,128]{3,2,1,0:T(8,128)(2,1)S(1)}, u32[]{:S(2)}, u32[]{:S(2)}) async-start(bf16[128,1,8,128]{3,2,1,0:T(8,128)(2,1)} %copy.76), calls=%async_computation.1 | async-start | bytes 524288 | tf_op jit(solution)/shard_map/all_to_all | solution.py:64
  22.5 12.2 %all-to-all-start = ((bf16[128,1,8,128]{3,2,1,0:T(8,128)(2,1)}), bf16[128,1,8,128]{3,2,1,0:T(8,128)(2,1)S(1)}, u32[]{:S(2)}, u32[]{:S(2)}) async-start(bf16[128,1,8,128]{3,2,1,0:T(8,128)(2,1)} %copy.74), calls=%async_computation | async-start | bytes 524288 | tf_op jit(solution)/shard_map/all_to_all | solution.py:57
  38.3 5.2 %copy-start.3 = (f32[2,128]{1,0:T(2,128)S(1)}, f32[2,128]{1,0:T(2,128)}, u32[]{:S(2)}) copy-start(f32[2,128]{1,0:T(2,128)} %param.12) | copy-start | bytes 3076
  38.3 5.3 %copy-start = (bf16[128,8,128]{2,1,0:T(8,128)(2,1)S(1)}, bf16[128,8,128]{2,1,0:T(8,128)(2,1)}, u32[]{:S(2)}) copy-start(bf16[128,8,128]{2,1,0:T(8,128)(2,1)} %param.7) | copy-start | bytes 786436
  38.3 5.3 %copy-start.4 = (bf16[2,128,128]{2,1,0:T(8,128)(2,1)S(1)}, bf16[2,128,128]{2,1,0:T(8,128)(2,1)}, u32[]{:S(2)}) copy-start(bf16[2,128,128]{2,1,0:T(8,128)(2,1)} %param.11) | copy-start | bytes 196612
  39.8 12.8 %copy-start.2 = (bf16[2,128,128]{2,1,0:T(8,128)(2,1)S(1)}, bf16[2,128,128]{2,1,0:T(8,128)(2,1)}, u32[]{:S(2)}) copy-start(bf16[2,128,128]{2,1,0:T(8,128)(2,1)} %param.13) | copy-start | bytes 196612
  39.8 12.2 %all-to-all-start.2 = ((bf16[16,8,8,128]{3,2,0,1:T(8,128)(2,1)}), bf16[16,8,8,128]{3,2,0,1:T(8,128)(2,1)S(1)}, u32[]{:S(2)}, u32[]{:S(2)}) async-start(bf16[16,8,8,128]{3,2,0,1:T(8,128)(2,1)} %copy.79), calls=%async_computation.2 | async-start | bytes 524288 | tf_op jit(solution)/shard_map/all_to_all | solution.py:103
  44.0 8.9 %copy-start.1 = (bf16[2,128,512]{2,1,0:T(8,128)(2,1)S(1)}, bf16[2,128,512]{2,1,0:T(8,128)(2,1)}, u32[]{:S(2)}) copy-start(bf16[2,128,512]{2,1,0:T(8,128)(2,1)} %param.10) | copy-start | bytes 786436
  54.7 12.0 %all-to-all-start.3 = ((bf16[128,1,8,128]{3,2,1,0:T(8,128)(2,1)}), bf16[128,1,8,128]{3,2,1,0:T(8,128)(2,1)S(1)}, u32[]{:S(2)}, u32[]{:S(2)}) async-start(bf16[128,1,8,128]{3,2,1,0:T(8,128)(2,1)} %copy.85), calls=%async_computation.3 | async-start | bytes 524288 | tf_op jit(solution)/shard_map/all_to_all | solution.py:57
  66.7 12.1 %all-to-all-start.4 = ((bf16[128,1,8,128]{3,2,1,0:T(8,128)(2,1)}), bf16[128,1,8,128]{3,2,1,0:T(8,128)(2,1)S(1)}, u32[]{:S(2)}, u32[]{:S(2)}) async-start(bf16[128,1,8,128]{3,2,1,0:T(8,128)(2,1)} %copy.88), calls=%async_computation.4 | async-start | bytes 524288 | tf_op jit(solution)/shard_map/all_to_all | solution.py:64
  82.1 15.2 %all-to-all-start.5 = ((bf16[16,8,8,128]{3,2,0,1:T(8,128)(2,1)}), bf16[16,8,8,128]{3,2,0,1:T(8,128)(2,1)S(1)}, u32[]{:S(2)}, u32[]{:S(2)}) async-start(bf16[16,8,8,128]{3,2,0,1:T(8,128)(2,1)} %copy.91), calls=%async_computation.5 | async-start | bytes 524288 | tf_op jit(solution)/shard_map/all_to_all | solution.py:103
where the time goes:
time: 100 us; the launch traced here: 99 us
  waiting for transfers between devices  38.8 us (39%)
  starting transfers between devices  27.5 us (28%)
  local copies, waits for them, and re-layouts  17.5 us (18%)
  blocking collectives  6.55 us (7%)
  other arithmetic  4.46 us (4%)
  matrix products  3.9 us (4%)
    all_to_all x2, waiting for transfers between devices, body(): lax.all_to_all(arranged, ('row', 'ch'), split_axis=1, concat_axis=0, tile...  16.8 us
    all_to_all x2, waiting for transfers between devices, body(): lax.all_to_all(left_proj.reshape(hidden, 1, local_rows, local_cols), ('ro...  14 us
    all_to_all x2, starting transfers between devices, body(): lax.all_to_all(right_proj.reshape(hidden, 1, local_rows, local_cols), ('r...  10.7 us
    all_to_all x2, starting transfers between devices, body(): lax.all_to_all(arranged, ('row', 'ch'), split_axis=1, concat_axis=0, tile...  9.72 us
    all_to_all x2, waiting for transfers between devices, body(): lax.all_to_all(right_proj.reshape(hidden, 1, local_rows, local_cols), ('r...  8.05 us
    all_to_all x2, starting transfers between devices, body(): lax.all_to_all(left_proj.reshape(hidden, 1, local_rows, local_cols), ('ro...  7.08 us
    convert_element_type x2, local copies, waits for them, and re-layouts, body(): result.reshape(per_device, used_rows, length).astype(jnp.bfloat16)  4.84 us
    all_gather x1, local copies, waits for them, and re-layouts, body(): shard_left = lax.all_gather(left_stack, 'sub', axis=2, tiled=True)  3.19 us
  transfers between devices with their start and end apart: 6, of which 5 were waited for; matrix products, arithmetic and copies ran while one was open for 9% of the time, Pallas kernels for 0%

commit v1 on v0

--- a/solution.py
+++ b/solution.py
@@ -1,9 +1,16 @@
+import functools
+
 import jax
 import jax.numpy as jnp
 from jax import lax
+from jax.experimental import pallas as pl
+from jax.experimental.pallas import tpu as pltpu
 from jax.sharding import PartitionSpec as P
 
 EPS = 1e-05
+MESH = pl.DeviceIdType.MESH
+F32 = jnp.float32
+BF16 = jnp.bfloat16
 
 
 def channel_norm(values, gain_vector):
@@ -13,7 +20,7 @@
     return centred * lax.rsqrt(spread + EPS) * gain_vector[:, None, None]
 
 
-def body(
+def split_body(
     pair_field, residue_mask, input_gain, projection_weight, gate_weight, output_gain, output_weight
 ):
     rows_count = lax.axis_size("row")
@@ -112,6 +119,261 @@
     return current
 
 
+def transposed(block):
+    return block.astype(F32).T
+
+
+def standardise(ref):
+    channels = ref.shape[0]
+    average = jnp.sum(ref[...], axis=0, keepdims=True) / channels
+    spread = jnp.sum(jnp.square(ref[...] - average), axis=0, keepdims=True) / channels
+    ref[...] = (ref[...] - average) * lax.rsqrt(spread + EPS)
+
+
+def kernel(
+    rows_count, halves,
+    pair, mask, gain_in, w_proj, w_gate, gain_out, w_out, out,
+    current, stage, wt, wg, wo, gcol, normed, gate, pair_mask, halfstage,
+    send, recv, msend, mrecv,
+    send_sem, recv_sem, msend_sem, mrecv_sem,
+):
+    devices = rows_count * halves
+    channels, local_rows, cols = pair.shape
+    own = channels // devices
+    pack = own * halves
+    row, sub = lax.axis_index("row"), lax.axis_index("sub")
+    me = row * halves + sub
+
+    def place(device):
+        return {"row": device // halves, "sub": device % halves}
+
+    barrier = pltpu.get_barrier_semaphore()
+
+    def greet(step, carry):
+        pl.semaphore_signal(
+            barrier, inc=1, device_id=place((me + step) % devices), device_id_type=MESH
+        )
+        return carry
+
+    lax.fori_loop(1, devices, greet, 0)
+
+    current[...] = pair[...].astype(F32)
+    for update in range(2):
+        for kind in range(4):
+            block = transposed(w_proj[update, :, kind * channels : (kind + 1) * channels])
+            wt[update, :, kind * pack : (kind + 1) * pack, :] = block.reshape(
+                rows_count, pack, channels
+            ).astype(BF16)
+        wg[update] = transposed(w_gate[update]).astype(BF16)
+        wo[update] = transposed(w_out[update]).astype(BF16)
+        gcol[2 * update] = jnp.broadcast_to(gain_in[update : update + 1, :], (cols, channels)).T
+        gcol[2 * update + 1] = jnp.broadcast_to(
+            gain_out[update : update + 1, :], (cols, channels)
+        ).T
+    col_mask = mask[...].astype(F32)
+    lane = lax.broadcasted_iota(jnp.int32, col_mask.shape, 1)
+    for r in range(local_rows):
+        mine = jnp.sum(
+            jnp.where(lane == me * local_rows + r, col_mask, 0.0), axis=1, keepdims=True
+        )
+        pair_mask[0:1, r * cols : (r + 1) * cols] = col_mask * mine
+
+    def lr_copy(update, device, slot):
+        return pltpu.make_async_remote_copy(
+            src_ref=send.at[update, device],
+            dst_ref=recv.at[update, slot],
+            send_sem=send_sem.at[update, device],
+            recv_sem=recv_sem.at[update, slot],
+            device_id=place(device),
+            device_id_type=MESH,
+        )
+
+    def m_copy(update, device, slot):
+        return pltpu.make_async_remote_copy(
+            src_ref=msend.at[update, device],
+            dst_ref=mrecv.at[update, slot],
+            send_sem=msend_sem.at[update, device],
+            recv_sem=mrecv_sem.at[update, slot],
+            device_id=place(device),
+            device_id_type=MESH,
+        )
+
+    for update in range(2):
+        stage[...] = current[...]
+        standardise(stage)
+        for r in range(local_rows):
+            normed[:, r * cols : (r + 1) * cols] = (stage[:, r, :] * gcol[2 * update]).astype(BF16)
+
+        def project(chip):
+            for part in range(local_rows // 2):
+                span = slice(part * 2 * cols, (part + 1) * 2 * cols)
+                values = jnp.dot(wt[update, chip], normed[:, span], preferred_element_type=F32)
+                masked = pair_mask[0:1, span]
+                for side in range(2):
+                    base = 2 * side * pack
+                    scaled = (
+                        masked
+                        * jax.nn.sigmoid(values[base + pack : base + 2 * pack])
+                        * values[base : base + pack]
+                    )
+                    for r in range(2):
+                        halfstage[side, :, part * 2 + r, :] = scaled[:, r * cols : (r + 1) * cols]
+            for half in range(halves):
+                for side in range(2):
+                    send[update, chip * halves + half, side] = (
+                        halfstage[side, half * own : (half + 1) * own]
+                        .reshape(own * local_rows, cols)
+                        .astype(BF16)
+                    )
+
+        if update == 0:
+            pl.semaphore_wait(barrier, devices - 1)
+
+        def chip_step(step, carry):
+            chip = (row + step) % rows_count
+            project(chip)
+            for half in range(halves):
+                lr_copy(update, chip * halves + half, me).start()
+            return carry
+
+        lax.fori_loop(1, rows_count, chip_step, 0)
+        project(row)
+        for half in range(1, halves):
+            lr_copy(update, row * halves + (sub + half) % halves, me).start()
+        recv[update, me] = send[update, me]
+        for part in range(local_rows // 2):
+            span = slice(part * 2 * cols, (part + 1) * 2 * cols)
+            gate[:, span] = jax.nn.sigmoid(
+                jnp.dot(wg[update], normed[:, span], preferred_element_type=F32)
+            )
+
+        def lr_arrived(step, carry):
+            device = (me + step) % devices
+            lr_copy(update, device, device).wait_recv()
+            return carry
+
+        lax.fori_loop(1, devices, lr_arrived, 0)
+
+        length = devices * local_rows
+        contract = ((1,), (1,)) if update == 0 else ((0,), (0,))
+        for couple in range(own // 2):
+            span = slice(couple * 2 * local_rows, (couple + 1) * 2 * local_rows)
+            sides = [
+                recv[update, :, side, span, :].astype(F32).reshape(devices, 2, local_rows, cols)
+                for side in range(2)
+            ]
+            products = []
+            for c in range(2):
+                left, right = (
+                    values[:, c].reshape(length, cols).astype(BF16) for values in sides
+                )
+                product = lax.dot_general(left, right, (contract, ((), ())), preferred_element_type=F32)
+                products.append(product.reshape(devices, 1, local_rows, cols))
+            msend[update, :, span, :] = (
+                jnp.concatenate(products, axis=1)
+                .reshape(devices, 2 * local_rows, cols)
+                .astype(BF16)
+            )
+
+        def m_step(step, carry):
+            m_copy(update, (me + step) % devices, me).start()
+            return carry
+
+        lax.fori_loop(1, devices, m_step, 0)
+        mrecv[update, me] = msend[update, me]
+
+        def m_arrived(step, carry):
+            device = (me + step) % devices
+            m_copy(update, device, device).wait_recv()
+            return carry
+
+        lax.fori_loop(1, devices, m_arrived, 0)
+
+        stage[...] = mrecv[update].astype(F32).reshape(channels, local_rows, cols)
+        standardise(stage)
+        for r in range(local_rows):
+            normed[:, r * cols : (r + 1) * cols] = (
+                stage[:, r, :] * gcol[2 * update + 1]
+            ).astype(BF16)
+        for part in range(local_rows // 2):
+            span = slice(part * 2 * cols, (part + 1) * 2 * cols)
+            term = gate[:, span] * jnp.dot(wo[update], normed[:, span], preferred_element_type=F32)
+            for r in range(2):
+                stage[:, part * 2 + r, :] = term[:, r * cols : (r + 1) * cols]
+        fresh = (current[...] + stage[...]).astype(BF16)
+        if update == 0:
+            current[...] = fresh.astype(F32)
+        else:
+            out[...] = fresh
+
+    def sent(step, carry):
+        device = (me + step) % devices
+        for update in range(2):
+            lr_copy(update, device, me).wait_send()
+            m_copy(update, device, me).wait_send()
+        return carry
+
+    lax.fori_loop(1, devices, sent, 0)
+
+
+def fused_body(rows_count, halves, pair, mask, gain_in, w_proj, w_gate, gain_out, w_out):
+    channels, local_rows, cols = pair.shape
+    devices = rows_count * halves
+    own = channels // devices
+    slab = own * local_rows
+    pack = own * halves
+    wide = local_rows * cols
+    vmem = pl.BlockSpec(memory_space=pltpu.VMEM)
+    return pl.pallas_call(
+        functools.partial(kernel, rows_count, halves),
+        out_shape=jax.ShapeDtypeStruct(pair.shape, BF16),
+        in_specs=[vmem] * 7,
+        out_specs=vmem,
+        scratch_shapes=[
+            pltpu.VMEM(pair.shape, F32),
+            pltpu.VMEM(pair.shape, F32),
+            pltpu.VMEM((2, rows_count, 4 * pack, channels), BF16),
+            pltpu.VMEM((2, channels, channels), BF16),
+            pltpu.VMEM((2, channels, channels), BF16),
+            pltpu.VMEM((4, channels, cols), F32),
+            pltpu.VMEM((channels, wide), BF16),
+            pltpu.VMEM((channels, wide), F32),
+            pltpu.VMEM((8, wide), F32),
+            pltpu.VMEM((2, pack, local_rows, cols), F32),
+            pltpu.VMEM((2, devices, 2, slab, cols), BF16),
+            pltpu.VMEM((2, devices, 2, slab, cols), BF16),
+            pltpu.VMEM((2, devices, slab, cols), BF16),
+            pltpu.VMEM((2, devices, slab, cols), BF16),
+            pltpu.SemaphoreType.DMA((2, devices)),
+            pltpu.SemaphoreType.DMA((2, devices)),
+            pltpu.SemaphoreType.DMA((2, devices)),
+            pltpu.SemaphoreType.DMA((2, devices)),
+        ],
+        compiler_params=pltpu.CompilerParams(
+            collective_id=0, has_side_effects=True, vmem_limit_bytes=32 * 2**20
+        ),
+    )(pair, mask.reshape(1, -1), gain_in, w_proj, w_gate, gain_out, w_out)
+
+
+def body(*args):
+    rows_count, halves = lax.axis_size("row"), lax.axis_size("sub")
+    channels, local_rows, cols = args[0].shape
+    hidden = args[6].shape[1]
+    devices = rows_count * halves
+    fits = (
+        lax.axis_size("ch") == 1
+        and hidden == channels
+        and devices > 1
+        and local_rows == 8
+        and cols == devices * local_rows
+        and channels == devices * 8
+        and cols % 128 == 0
+    )
+    if fits:
+        return fused_body(rows_count, halves, *args)
+    return split_body(*args)
+
+
 def solution(mesh):
     placed = (P(None, ("grp", "row", "sub"), "ch"), P("grp"), P(), P(), P(), P(), P())
     return jax.shard_map(

time: 100 us -> 55.9 us (0.56)
  Pallas kernels: 0 us -> 50 us
  waiting for transfers between devices: 38.8 us -> 0 us
  starting transfers between devices: 27.5 us -> 0 us
  local copies, waits for them, and re-layouts: 17.5 us -> 5.64 us
  blocking collectives: 6.55 us -> 0 us
  other arithmetic: 4.46 us -> 0 us
  matrix products: 3.9 us -> 0 us
    pallas_call x0 -> x1, Pallas kernels: none -> 50 us  [fused_body(): pl.pallas_call(functools.partial(kernel, rows_count, halves), out_shape=j...]
    all_to_all x6 -> x0, waiting for transfers between devices: 38.8 us -> none  [the longest x2 16.8 us: body(): lax.all_to_all(arranged, ('row', 'ch'), split_axis=1, concat_axis=0, tile...]
    all_to_all x6 -> x0, starting transfers between devices: 27.5 us -> none  [the longest x2 10.7 us: body(): lax.all_to_all(right_proj.reshape(hidden, 1, local_rows, local_cols), ('r...]
    reshape x6 -> x0, local copies, waits for them, and re-layouts: 6.64 us -> none  [the longest x2 3.14 us: body(): chosen.reshape(per_device, rows_count, span_count, local_rows, used_rows)]
    all_gather x3 -> x0, blocking collectives: 6.55 us -> none  [the longest x1 2.18 us: body(): lax.all_gather(stacked, 'sub', axis=2, tiled=True)]
    convert_element_type x3 -> x0, local copies, waits for them, and re-layouts: 5.72 us -> none  [the longest x2 4.84 us: body(): result.reshape(per_device, used_rows, length).astype(jnp.bfloat16)]
    unnamed x10 -> x15, local copies, waits for them, and re-layouts: 0.03 us -> 5.64 us
    dot_general x8 -> x0, matrix products: 3.9 us -> none  [the longest x2 2.03 us: body(): jnp.einsum('dpq,de->epq', normed, projection_weight[update], preferred_el...]
  transfers between devices with their start and end apart: 6 -> 0, of which waited for: 5 -> 0; matrix products, arithmetic and copies ran while one was open for 9% -> 0% of each run, Pallas kernels for 0% -> 0%
where the time goes in v1:
time: 55.9 us; the launch traced here: 55.6 us
  Pallas kernels  50 us (89%)
  local copies, waits for them, and re-layouts  5.64 us (10%)
    pallas_call x1, Pallas kernels, fused_body(): pl.pallas_call(functools.partial(kernel, rows_count, halves), out_shape=j...  50 us
    unnamed x15, local copies, waits for them, and re-layouts  5.64 us

profile of v1, /device:TPU:0, one launch (start us, length us, event | category | flops | bytes accessed | tf_op | source)
XLA Modules:
  0.0 55.6 jit_solution(11931427838537273833)
XLA Ops:
  0.0 0.0 copy-start.4
  0.0 0.0 copy-start.6
  0.0 0.7 %copy-done.4 = f32[2,128]{1,0:T(2,128)S(1)} copy-done((f32[2,128]{1,0:T(2,128)S(1)}, f32[2,128]{1,0:T(2,128)}, u32[]{:S(2)}) %copy-start.4) | copy-done | bytes 1048
  0.7 0.0 copy-done.6
  0.7 0.0 copy-start
  0.7 0.9 %copy-done = bf16[128,8,128]{2,1,0:T(8,128)(2,1)S(1)} copy-done((bf16[128,8,128]{2,1,0:T(8,128)(2,1)S(1)}, bf16[128,8,128]{2,1,0:T(8,128)(2,1)}, u32[]{:S(2)}) %copy-start) | copy-done | bytes 262168
  1.6 0.0 copy-start.1
  1.6 0.9 %copy-done.1 = bf16[2,128,512]{2,1,0:T(8,128)(2,1)S(1)} copy-done((bf16[2,128,512]{2,1,0:T(8,128)(2,1)S(1)}, bf16[2,128,512]{2,1,0:T(8,128)(2,1)}, u32[]{:S(2)}) %copy-start.1) | copy-done | bytes 262168
  2.6 0.0 copy-start.2
  2.6 0.8 %copy-done.2 = bf16[2,128,128]{2,1,0:T(8,128)(2,1)S(1)} copy-done((bf16[2,128,128]{2,1,0:T(8,128)(2,1)S(1)}, bf16[2,128,128]{2,1,0:T(8,128)(2,1)}, u32[]{:S(2)}) %copy-start.2) | copy-done | bytes 65560
  3.4 0.0 copy-start.3
  3.4 0.8 %copy-done.3 = bf16[2,128,128]{2,1,0:T(8,128)(2,1)S(1)} copy-done((bf16[2,128,128]{2,1,0:T(8,128)(2,1)S(1)}, bf16[2,128,128]{2,1,0:T(8,128)(2,1)}, u32[]{:S(2)}) %copy-start.3) | copy-done | bytes 65560
  4.3 0.0 copy-start.5
  4.3 0.7 %copy-done.5 = f32[2,128]{1,0:T(2,128)S(1)} copy-done((f32[2,128]{1,0:T(2,128)S(1)}, f32[2,128]{1,0:T(2,128)}, u32[]{:S(2)}) %copy-start.5) | copy-done | bytes 1048
  4.9 50.0 %shard_map.73 = bf16[128,8,128]{2,1,0:T(8,128)(2,1)S(1)} custom-call(bf16[128,8,128]{2,1,0:T(8,128)(2,1)S(1)} %copy-done, s32[1,128]{1,0:T(1,128)S(1)} %bitcast.1, f32[2,128]{1,0:T(2,128)S(1)} %copy-done.4, bf16[2,128,512]{2,1,0:T(8,128)(2,1)S(1)} %copy-done.1, bf16[2,128,128]{2,1,0:T(8,128)(2,1)S(1)} %copy-done.2, f32[2,128]{1,0:T(2,128)S(1)} %copy-done.5, ...), custom_call_target="tpu_custom_call" | custom-call | tf_op jit(solution)/shard_map/pallas_call | solution.py:327
  54.9 0.7 %copy.9 = bf16[128,8,128]{2,1,0:T(8,128)(2,1)} copy(bf16[128,8,128]{2,1,0:T(8,128)(2,1)S(1)} %shard_map.73) | data formatting | bytes 524288
Async XLA Ops:
  0.0 0.7 %copy-start.4 = (f32[2,128]{1,0:T(2,128)S(1)}, f32[2,128]{1,0:T(2,128)}, u32[]{:S(2)}) copy-start(f32[2,128]{1,0:T(2,128)} %gain_in.1) | copy-start | bytes 3076
  0.0 0.7 %copy-start.6 = (s32[128]{0:T(128)S(1)}, s32[128]{0:T(128)}, u32[]{:S(2)}) copy-start(s32[128]{0:T(128)} %param.8) | copy-start | bytes 1540
  0.7 1.0 %copy-start = (bf16[128,8,128]{2,1,0:T(8,128)(2,1)S(1)}, bf16[128,8,128]{2,1,0:T(8,128)(2,1)}, u32[]{:S(2)}) copy-start(bf16[128,8,128]{2,1,0:T(8,128)(2,1)} %pair.1) | copy-start | bytes 786436
  1.6 0.9 %copy-start.1 = (bf16[2,128,512]{2,1,0:T(8,128)(2,1)S(1)}, bf16[2,128,512]{2,1,0:T(8,128)(2,1)}, u32[]{:S(2)}) copy-start(bf16[2,128,512]{2,1,0:T(8,128)(2,1)} %w_proj.1) | copy-start | bytes 786436
  2.6 0.8 %copy-start.2 = (bf16[2,128,128]{2,1,0:T(8,128)(2,1)S(1)}, bf16[2,128,128]{2,1,0:T(8,128)(2,1)}, u32[]{:S(2)}) copy-start(bf16[2,128,128]{2,1,0:T(8,128)(2,1)} %w_gate.1) | copy-start | bytes 196612
  3.4 0.8 %copy-start.3 = (bf16[2,128,128]{2,1,0:T(8,128)(2,1)S(1)}, bf16[2,128,128]{2,1,0:T(8,128)(2,1)}, u32[]{:S(2)}) copy-start(bf16[2,128,128]{2,1,0:T(8,128)(2,1)} %w_out.1) | copy-start | bytes 196612
  4.3 0.7 %copy-start.5 = (f32[2,128]{1,0:T(2,128)S(1)}, f32[2,128]{1,0:T(2,128)}, u32[]{:S(2)}) copy-start(f32[2,128]{1,0:T(2,128)} %gain_out.1) | copy-start | bytes 3076

commit v2 on v1

--- a/solution.py
+++ b/solution.py
@@ -123,26 +123,54 @@
     return block.astype(F32).T
 
 
-def standardise(ref):
-    channels = ref.shape[0]
-    average = jnp.sum(ref[...], axis=0, keepdims=True) / channels
-    spread = jnp.sum(jnp.square(ref[...] - average), axis=0, keepdims=True) / channels
-    ref[...] = (ref[...] - average) * lax.rsqrt(spread + EPS)
+def moments(ref):
+    channels, chunk = ref.shape[0], 16
+    total = jnp.zeros(ref.shape[1:], F32)
+    for start in range(0, channels, chunk):
+        total = total + jnp.sum(ref[start : start + chunk], axis=0)
+    average = total / channels
+    total = jnp.zeros(ref.shape[1:], F32)
+    for start in range(0, channels, chunk):
+        total = total + jnp.sum(jnp.square(ref[start : start + chunk] - average), axis=0)
+    return average, lax.rsqrt(total / channels + EPS)
 
 
 def kernel(
     rows_count, halves,
-    pair, mask, gain_in, w_proj, w_gate, gain_out, w_out, out,
-    current, stage, wt, wg, wo, gcol, normed, gate, pair_mask, halfstage,
+    pair_hbm, mask_hbm, gain_in_hbm, w_proj_hbm, w_gate_hbm, gain_out_hbm, w_out_hbm, out,
+    pair, mask, gain_in, w_proj, w_gate, gain_out, w_out,
+    current, stage, wt, wg, wo, gcol, normed, gate, pair_mask, slab_stage,
     send, recv, msend, mrecv,
-    send_sem, recv_sem, msend_sem, mrecv_sem,
+    in_sem, send_sem, recv_sem, msend_sem, mrecv_sem,
 ):
     devices = rows_count * halves
     channels, local_rows, cols = pair.shape
-    own = channels // devices
-    pack = own * halves
+    plane = 4
+    planes = devices // plane
+    own = channels // devices // 2
+    pack = own * plane
+    half_channels = channels // 2
     row, sub = lax.axis_index("row"), lax.axis_index("sub")
     me = row * halves + sub
+    my_plane = me // plane
+    my_seat = me % plane
+
+    fetches = [
+        pltpu.make_async_copy(src, dst, in_sem.at[index])
+        for index, (src, dst) in enumerate(
+            (
+                (pair_hbm, pair),
+                (w_proj_hbm, w_proj),
+                (gain_in_hbm, gain_in),
+                (mask_hbm, mask),
+                (w_gate_hbm, w_gate),
+                (gain_out_hbm, gain_out),
+                (w_out_hbm, w_out),
+            )
+        )
+    ]
+    for fetch in fetches:
+        fetch.start()
 
     def place(device):
         return {"row": device // halves, "sub": device % halves}
@@ -157,19 +185,24 @@
 
     lax.fori_loop(1, devices, greet, 0)
 
-    current[...] = pair[...].astype(F32)
-    for update in range(2):
+    def prepare_projection(update):
         for kind in range(4):
             block = transposed(w_proj[update, :, kind * channels : (kind + 1) * channels])
             wt[update, :, kind * pack : (kind + 1) * pack, :] = block.reshape(
-                rows_count, pack, channels
+                2 * planes, pack, channels
             ).astype(BF16)
-        wg[update] = transposed(w_gate[update]).astype(BF16)
+        gcol[2 * update] = jnp.broadcast_to(gain_in[update : update + 1, :], (cols, channels)).T
+
+    def prepare_finish(update):
         wo[update] = transposed(w_out[update]).astype(BF16)
-        gcol[2 * update] = jnp.broadcast_to(gain_in[update : update + 1, :], (cols, channels)).T
         gcol[2 * update + 1] = jnp.broadcast_to(
             gain_out[update : update + 1, :], (cols, channels)
         ).T
+
+    for fetch in fetches[:4]:
+        fetch.wait()
+    current[...] = pair[...].astype(F32)
+    prepare_projection(0)
     col_mask = mask[...].astype(F32)
     lane = lax.broadcasted_iota(jnp.int32, col_mask.shape, 1)
     for r in range(local_rows):
@@ -178,36 +211,42 @@
         )
         pair_mask[0:1, r * cols : (r + 1) * cols] = col_mask * mine
 
-    def lr_copy(update, device, slot):
+    def lr_copy(update, half, device, slot):
         return pltpu.make_async_remote_copy(
-            src_ref=send.at[update, device],
-            dst_ref=recv.at[update, slot],
-            send_sem=send_sem.at[update, device],
-            recv_sem=recv_sem.at[update, slot],
+            src_ref=send.at[update, half, device],
+            dst_ref=recv.at[update, half, slot],
+            send_sem=send_sem.at[update, half, device],
+            recv_sem=recv_sem.at[update, half, slot],
             device_id=place(device),
             device_id_type=MESH,
         )
 
-    def m_copy(update, device, slot):
+    def m_copy(update, half, device, slot):
         return pltpu.make_async_remote_copy(
-            src_ref=msend.at[update, device],
-            dst_ref=mrecv.at[update, slot],
-            send_sem=msend_sem.at[update, device],
-            recv_sem=mrecv_sem.at[update, slot],
+            src_ref=msend.at[update, half, device],
+            dst_ref=mrecv.at[update, half, slot],
+            send_sem=msend_sem.at[update, half, device],
+            recv_sem=mrecv_sem.at[update, half, slot],
             device_id=place(device),
             device_id_type=MESH,
         )
 
+    def normalise(ref, gains):
+        average, scale = moments(ref)
+        for r in range(local_rows):
+            normed[:, r * cols : (r + 1) * cols] = (
+                (ref[:, r, :] - average[r : r + 1]) * scale[r : r + 1] * gcol[gains]
+            ).astype(BF16)
+
     for update in range(2):
-        stage[...] = current[...]
-        standardise(stage)
-        for r in range(local_rows):
-            normed[:, r * cols : (r + 1) * cols] = (stage[:, r, :] * gcol[2 * update]).astype(BF16)
-
-        def project(chip):
+        normalise(current, 2 * update)
+
+        def project(half, group):
             for part in range(local_rows // 2):
                 span = slice(part * 2 * cols, (part + 1) * 2 * cols)
-                values = jnp.dot(wt[update, chip], normed[:, span], preferred_element_type=F32)
+                values = jnp.dot(
+                    wt[update, half * planes + group], normed[:, span], preferred_element_type=F32
+                )
                 masked = pair_mask[0:1, span]
                 for side in range(2):
                     base = 2 * side * pack
@@ -217,11 +256,11 @@
                         * values[base : base + pack]
                     )
                     for r in range(2):
-                        halfstage[side, :, part * 2 + r, :] = scaled[:, r * cols : (r + 1) * cols]
-            for half in range(halves):
+                        slab_stage[side, :, part * 2 + r, :] = scaled[:, r * cols : (r + 1) * cols]
+            for seat in range(plane):
                 for side in range(2):
-                    send[update, chip * halves + half, side] = (
-                        halfstage[side, half * own : (half + 1) * own]
+                    send[update, half, group * plane + seat, side] = (
+                        slab_stage[side, seat * own : (seat + 1) * own]
                         .reshape(own * local_rows, cols)
                         .astype(BF16)
                     )
@@ -229,72 +268,89 @@
         if update == 0:
             pl.semaphore_wait(barrier, devices - 1)
 
-        def chip_step(step, carry):
-            chip = (row + step) % rows_count
-            project(chip)
-            for half in range(halves):
-                lr_copy(update, chip * halves + half, me).start()
-            return carry
-
-        lax.fori_loop(1, rows_count, chip_step, 0)
-        project(row)
-        for half in range(1, halves):
-            lr_copy(update, row * halves + (sub + half) % halves, me).start()
-        recv[update, me] = send[update, me]
+        for half in range(2):
+
+            def plane_step(step, carry):
+                group = (my_plane + step) % planes
+                project(half, group)
+                for seat in range(plane):
+                    lr_copy(update, half, group * plane + (my_seat + seat) % plane, me).start()
+                return carry
+
+            lax.fori_loop(1, planes, plane_step, 0)
+            project(half, my_plane)
+            for seat in range(1, plane):
+                lr_copy(update, half, my_plane * plane + (my_seat + seat) % plane, me).start()
+            recv[update, half, me] = send[update, half, me]
+
+        if update == 0:
+            for fetch in fetches[4:]:
+                fetch.wait()
+            for later in range(2):
+                wg[later] = transposed(w_gate[later]).astype(BF16)
         for part in range(local_rows // 2):
             span = slice(part * 2 * cols, (part + 1) * 2 * cols)
             gate[:, span] = jax.nn.sigmoid(
                 jnp.dot(wg[update], normed[:, span], preferred_element_type=F32)
             )
-
-        def lr_arrived(step, carry):
-            device = (me + step) % devices
-            lr_copy(update, device, device).wait_recv()
-            return carry
-
-        lax.fori_loop(1, devices, lr_arrived, 0)
+        if update == 0:
+            prepare_finish(0)
+            prepare_projection(1)
+            prepare_finish(1)
 
         length = devices * local_rows
         contract = ((1,), (1,)) if update == 0 else ((0,), (0,))
-        for couple in range(own // 2):
-            span = slice(couple * 2 * local_rows, (couple + 1) * 2 * local_rows)
-            sides = [
-                recv[update, :, side, span, :].astype(F32).reshape(devices, 2, local_rows, cols)
-                for side in range(2)
-            ]
-            products = []
-            for c in range(2):
-                left, right = (
-                    values[:, c].reshape(length, cols).astype(BF16) for values in sides
+        for half in range(2):
+
+            def lr_arrived(step, carry):
+                device = (me + step) % devices
+                lr_copy(update, half, device, device).wait_recv()
+                return carry
+
+            lax.fori_loop(1, devices, lr_arrived, 0)
+            for couple in range(own // 2):
+                span = slice(couple * 2 * local_rows, (couple + 1) * 2 * local_rows)
+                sides = [
+                    recv[update, half, :, side, span, :]
+                    .astype(F32)
+                    .reshape(devices, 2, local_rows, cols)
+                    for side in range(2)
+                ]
+                products = []
+                for c in range(2):
+                    left, right = (
+                        values[:, c].reshape(length, cols).astype(BF16) for values in sides
+                    )
+                    product = lax.dot_general(
+                        left, right, (contract, ((), ())), preferred_element_type=F32
+                    )
+                    products.append(product.reshape(devices, 1, local_rows, cols))
+                msend[update, half, :, span, :] = (
+                    jnp.concatenate(products, axis=1)
+                    .reshape(devices, 2 * local_rows, cols)
+                    .astype(BF16)
                 )
-                product = lax.dot_general(left, right, (contract, ((), ())), preferred_element_type=F32)
-                products.append(product.reshape(devices, 1, local_rows, cols))
-            msend[update, :, span, :] = (
-                jnp.concatenate(products, axis=1)
-                .reshape(devices, 2 * local_rows, cols)
-                .astype(BF16)
-            )
-
-        def m_step(step, carry):
-            m_copy(update, (me + step) % devices, me).start()
-            return carry
-
-        lax.fori_loop(1, devices, m_step, 0)
-        mrecv[update, me] = msend[update, me]
-
-        def m_arrived(step, carry):
-            device = (me + step) % devices
-            m_copy(update, device, device).wait_recv()
-            return carry
-
-        lax.fori_loop(1, devices, m_arrived, 0)
-
-        stage[...] = mrecv[update].astype(F32).reshape(channels, local_rows, cols)
-        standardise(stage)
-        for r in range(local_rows):
-            normed[:, r * cols : (r + 1) * cols] = (
-                stage[:, r, :] * gcol[2 * update + 1]
-            ).astype(BF16)
+
+            def m_step(step, carry):
+                m_copy(update, half, (me + step) % devices, me).start()
+                return carry
+
+            lax.fori_loop(1, devices, m_step, 0)
+            mrecv[update, half, me] = msend[update, half, me]
+
+        for half in range(2):
+
+            def m_arrived(step, carry):
+                device = (me + step) % devices
+                m_copy(update, half, device, device).wait_recv()
+                return carry
+
+            lax.fori_loop(1, devices, m_arrived, 0)
+            stage[half * half_channels : (half + 1) * half_channels] = (
+                mrecv[update, half].astype(F32).reshape(half_channels, local_rows, cols)
+            )
+
+        normalise(stage, 2 * update + 1)
         for part in range(local_rows // 2):
             span = slice(part * 2 * cols, (part + 1) * 2 * cols)
             term = gate[:, span] * jnp.dot(wo[update], normed[:, span], preferred_element_type=F32)
@@ -309,8 +365,9 @@
     def sent(step, carry):
         device = (me + step) % devices
         for update in range(2):
-            lr_copy(update, device, me).wait_send()
-            m_copy(update, device, me).wait_send()
+            for half in range(2):
+                lr_copy(update, half, device, me).wait_send()
+                m_copy(update, half, device, me).wait_send()
         return carry
 
     lax.fori_loop(1, devices, sent, 0)
@@ -319,20 +376,23 @@
 def fused_body(rows_count, halves, pair, mask, gain_in, w_proj, w_gate, gain_out, w_out):
     channels, local_rows, cols = pair.shape
     devices = rows_count * halves
-    own = channels // devices
+    own = channels // devices // 2
     slab = own * local_rows
-    pack = own * halves
+    pack = own * 4
     wide = local_rows * cols
+    operands = (pair, mask.reshape(1, -1), gain_in, w_proj, w_gate, gain_out, w_out)
     vmem = pl.BlockSpec(memory_space=pltpu.VMEM)
+    hbm = pl.BlockSpec(memory_space=pltpu.HBM)
     return pl.pallas_call(
         functools.partial(kernel, rows_count, halves),
         out_shape=jax.ShapeDtypeStruct(pair.shape, BF16),
-        in_specs=[vmem] * 7,
+        in_specs=[hbm] * 7,
         out_specs=vmem,
-        scratch_shapes=[
+        scratch_shapes=[pltpu.VMEM(each.shape, each.dtype) for each in operands]
+        + [
             pltpu.VMEM(pair.shape, F32),
             pltpu.VMEM(pair.shape, F32),
-            pltpu.VMEM((2, rows_count, 4 * pack, channels), BF16),
+            pltpu.VMEM((2, devices // 2, 4 * pack, channels), BF16),
             pltpu.VMEM((2, channels, channels), BF16),
             pltpu.VMEM((2, channels, channels), BF16),
             pltpu.VMEM((4, channels, cols), F32),
@@ -340,19 +400,20 @@
             pltpu.VMEM((channels, wide), F32),
             pltpu.VMEM((8, wide), F32),
             pltpu.VMEM((2, pack, local_rows, cols), F32),
-            pltpu.VMEM((2, devices, 2, slab, cols), BF16),
-            pltpu.VMEM((2, devices, 2, slab, cols), BF16),
-            pltpu.VMEM((2, devices, slab, cols), BF16),
-            pltpu.VMEM((2, devices, slab, cols), BF16),
-            pltpu.SemaphoreType.DMA((2, devices)),
-            pltpu.SemaphoreType.DMA((2, devices)),
-            pltpu.SemaphoreType.DMA((2, devices)),
-            pltpu.SemaphoreType.DMA((2, devices)),
+            pltpu.VMEM((2, 2, devices, 2, slab, cols), BF16),
+            pltpu.VMEM((2, 2, devices, 2, slab, cols), BF16),
+            pltpu.VMEM((2, 2, devices, slab, cols), BF16),
+            pltpu.VMEM((2, 2, devices, slab, cols), BF16),
+            pltpu.SemaphoreType.DMA((7,)),
+            pltpu.SemaphoreType.DMA((2, 2, devices)),
+            pltpu.SemaphoreType.DMA((2, 2, devices)),
+            pltpu.SemaphoreType.DMA((2, 2, devices)),
+            pltpu.SemaphoreType.DMA((2, 2, devices)),
         ],
         compiler_params=pltpu.CompilerParams(
-            collective_id=0, has_side_effects=True, vmem_limit_bytes=32 * 2**20
+            collective_id=0, has_side_effects=True, vmem_limit_bytes=60 * 2**20
         ),
-    )(pair, mask.reshape(1, -1), gain_in, w_proj, w_gate, gain_out, w_out)
+    )(*operands)
 
 
 def body(*args):
@@ -363,7 +424,7 @@
     fits = (
         lax.axis_size("ch") == 1
         and hidden == channels
-        and devices > 1
+        and devices % 4 == 0
         and local_rows == 8
         and cols == devices * local_rows
         and channels == devices * 8

time: 55.9 us -> 53.6 us (0.959)
  local copies, waits for them, and re-layouts: 5.64 us -> 1.67 us
  Pallas kernels: 50 us -> 51.8 us
    unnamed x15 -> x1, local copies, waits for them, and re-layouts: 5.64 us -> 1.67 us
    pallas_call x1, Pallas kernels: 50 us -> 51.8 us  [fused_body(): pl.pallas_call(functools.partial(kernel, rows_count, halves), out_shape=j...]
where the time goes in v2:
time: 53.6 us; the launch traced here: 53.5 us
  Pallas kernels  51.8 us (97%)
  local copies, waits for them, and re-layouts  1.67 us (3%)
    pallas_call x1, Pallas kernels, fused_body(): pl.pallas_call(functools.partial(kernel, rows_count, halves), out_shape=j...  51.8 us
    unnamed x1, local copies, waits for them, and re-layouts  1.67 us

profile of v2, /device:TPU:0, one launch (start us, length us, event | category | flops | bytes accessed | tf_op | source)
XLA Modules:
  0.0 53.5 jit_solution(16321491478667835482)
XLA Ops:
  0.0 51.8 %shard_map.73 = bf16[128,8,128]{2,1,0:T(8,128)(2,1)} custom-call(bf16[128,8,128]{2,1,0:T(8,128)(2,1)} %pair_hbm.1, s32[1,128]{1,0:T(1,128)} %bitcast.1, f32[2,128]{1,0:T(2,128)} %gain_in_hbm.1, bf16[2,128,512]{2,1,0:T(8,128)(2,1)} %w_proj_hbm.1, bf16[2,128,128]{2,1,0:T(8,128)(2,1)} %w_gate_hbm.1, f32[2,128]{1,0:T(2,128)} %gain_out_hbm.1, ...), custom_call_target="tpu_custom_call" | custom-call | tf_op jit(solution)/shard_map/pallas_call | solution.py:386
  51.8 1.7 %copy.9 = bf16[128,8,128]{2,1,0:T(8,128)(2,1)} copy(bf16[128,8,128]{2,1,0:T(8,128)(2,1)} %shard_map.73) | data formatting | bytes 524288

commit v3 on v2

--- a/solution.py
+++ b/solution.py
@@ -140,20 +140,24 @@
     pair_hbm, mask_hbm, gain_in_hbm, w_proj_hbm, w_gate_hbm, gain_out_hbm, w_out_hbm, out,
     pair, mask, gain_in, w_proj, w_gate, gain_out, w_out,
     current, stage, wt, wg, wo, gcol, normed, gate, pair_mask, slab_stage,
-    send, recv, msend, mrecv,
-    in_sem, send_sem, recv_sem, msend_sem, mrecv_sem,
+    lsend, rsend, lrecv, rrecv, msend, mrecv,
+    in_sem, lsend_sem, lrecv_sem, rsend_sem, rrecv_sem, msend_sem, mrecv_sem,
 ):
     devices = rows_count * halves
     channels, local_rows, cols = pair.shape
+    camp = devices // 2
     plane = 4
-    planes = devices // plane
-    own = channels // devices // 2
+    planes = camp // plane
+    own = channels // camp // 2
     pack = own * plane
     half_channels = channels // 2
     row, sub = lax.axis_index("row"), lax.axis_index("sub")
     me = row * halves + sub
-    my_plane = me // plane
-    my_seat = me % plane
+    my_base = (me // camp) * camp
+    far_base = camp - my_base
+    my_rank = me % camp
+    my_plane = my_rank // plane
+    my_seat = my_rank % plane
 
     fetches = [
         pltpu.make_async_copy(src, dst, in_sem.at[index])
@@ -211,12 +215,22 @@
         )
         pair_mask[0:1, r * cols : (r + 1) * cols] = col_mask * mine
 
-    def lr_copy(update, half, device, slot):
+    def l_copy(update, half, device, slot):
         return pltpu.make_async_remote_copy(
-            src_ref=send.at[update, half, device],
-            dst_ref=recv.at[update, half, slot],
-            send_sem=send_sem.at[update, half, device],
-            recv_sem=recv_sem.at[update, half, slot],
+            src_ref=lsend.at[update, half, device % camp],
+            dst_ref=lrecv.at[update, half, slot],
+            send_sem=lsend_sem.at[update, half, device % camp],
+            recv_sem=lrecv_sem.at[update, half, slot],
+            device_id=place(device),
+            device_id_type=MESH,
+        )
+
+    def r_copy(update, half, device, slot):
+        return pltpu.make_async_remote_copy(
+            src_ref=rsend.at[update, half, device % camp],
+            dst_ref=rrecv.at[update, half, slot],
+            send_sem=rsend_sem.at[update, half, device],
+            recv_sem=rrecv_sem.at[update, half, slot],
             device_id=place(device),
             device_id_type=MESH,
         )
@@ -258,8 +272,8 @@
                     for r in range(2):
                         slab_stage[side, :, part * 2 + r, :] = scaled[:, r * cols : (r + 1) * cols]
             for seat in range(plane):
-                for side in range(2):
-                    send[update, half, group * plane + seat, side] = (
+                for side, target in enumerate((lsend, rsend)):
+                    target[update, half, group * plane + seat] = (
                         slab_stage[side, seat * own : (seat + 1) * own]
                         .reshape(own * local_rows, cols)
                         .astype(BF16)
@@ -268,20 +282,20 @@
         if update == 0:
             pl.semaphore_wait(barrier, devices - 1)
 
+        r_slot = me if update == 0 else my_rank
         for half in range(2):
-
-            def plane_step(step, carry):
+            for step in range(1, planes + 1):
                 group = (my_plane + step) % planes
                 project(half, group)
                 for seat in range(plane):
-                    lr_copy(update, half, group * plane + (my_seat + seat) % plane, me).start()
-                return carry
-
-            lax.fori_loop(1, planes, plane_step, 0)
-            project(half, my_plane)
-            for seat in range(1, plane):
-                lr_copy(update, half, my_plane * plane + (my_seat + seat) % plane, me).start()
-            recv[update, half, me] = send[update, half, me]
+                    rank = group * plane + (my_seat + seat) % plane
+                    if update == 0:
+                        r_copy(update, half, far_base + rank, r_slot).start()
+                    if step < planes or seat > 0:
+                        l_copy(update, half, my_base + rank, my_rank).start()
+                        r_copy(update, half, my_base + rank, r_slot).start()
+            lrecv[update, half, my_rank] = lsend[update, half, my_rank]
+            rrecv[update, half, r_slot] = rsend[update, half, my_rank]
 
         if update == 0:
             for fetch in fetches[4:]:
@@ -298,56 +312,89 @@
             prepare_projection(1)
             prepare_finish(1)
 
-        length = devices * local_rows
         contract = ((1,), (1,)) if update == 0 else ((0,), (0,))
+        sources = devices if update == 0 else camp
+        targets = camp if update == 0 else devices
         for half in range(2):
 
-            def lr_arrived(step, carry):
-                device = (me + step) % devices
-                lr_copy(update, half, device, device).wait_recv()
+            def near_arrived(step, carry):
+                rank = (my_rank + step) % camp
+                l_copy(update, half, my_base + rank, rank).wait_recv()
+                slot = my_base + rank if update == 0 else rank
+                r_copy(update, half, my_base + rank, slot).wait_recv()
                 return carry
 
-            lax.fori_loop(1, devices, lr_arrived, 0)
+            lax.fori_loop(1, camp, near_arrived, 0)
+            if update == 0:
+
+                def far_arrived(step, carry):
+                    device = far_base + (my_rank + step) % camp
+                    r_copy(update, half, device, device).wait_recv()
+                    return carry
+
+                lax.fori_loop(0, camp, far_arrived, 0)
             for couple in range(own // 2):
                 span = slice(couple * 2 * local_rows, (couple + 1) * 2 * local_rows)
-                sides = [
-                    recv[update, half, :, side, span, :]
-                    .astype(F32)
-                    .reshape(devices, 2, local_rows, cols)
-                    for side in range(2)
-                ]
+                lefts = lrecv[update, half, :, span, :].astype(F32)
+                lefts = lefts.reshape(camp, 2, local_rows, cols)
+                rights = rrecv[update, half, :sources, span, :].astype(F32)
+                rights = rights.reshape(sources, 2, local_rows, cols)
                 products = []
                 for c in range(2):
-                    left, right = (
-                        values[:, c].reshape(length, cols).astype(BF16) for values in sides
+                    product = lax.dot_general(
+                        lefts[:, c].reshape(camp * local_rows, cols).astype(BF16),
+                        rights[:, c].reshape(sources * local_rows, cols).astype(BF16),
+                        (contract, ((), ())),
+                        preferred_element_type=F32,
                     )
-                    product = lax.dot_general(
-                        left, right, (contract, ((), ())), preferred_element_type=F32
-                    )
-                    products.append(product.reshape(devices, 1, local_rows, cols))
-                msend[update, half, :, span, :] = (
+                    products.append(product.reshape(targets, 1, local_rows, cols))
+                block = (
                     jnp.concatenate(products, axis=1)
-                    .reshape(devices, 2 * local_rows, cols)
+                    .reshape(targets, 2 * local_rows, cols)
                     .astype(BF16)
                 )
-
-            def m_step(step, carry):
-                m_copy(update, half, (me + step) % devices, me).start()
+                if update == 0:
+                    msend[update, half, pl.ds(my_base, camp), span, :] = block
+                else:
+                    msend[update, half, :, span, :] = block
+
+            if update == 1:
+
+                def m_far(step, carry):
+                    rank = (my_rank + step) % camp
+                    m_copy(update, half, far_base + rank, camp + my_rank).start()
+                    return carry
+
+                lax.fori_loop(0, camp, m_far, 0)
+
+            def m_near(step, carry):
+                rank = (my_rank + step) % camp
+                m_copy(update, half, my_base + rank, my_rank).start()
                 return carry
 
-            lax.fori_loop(1, devices, m_step, 0)
-            mrecv[update, half, me] = msend[update, half, me]
+            lax.fori_loop(1, camp, m_near, 0)
+            mrecv[update, half, my_rank] = msend[update, half, me]
 
         for half in range(2):
 
             def m_arrived(step, carry):
-                device = (me + step) % devices
-                m_copy(update, half, device, device).wait_recv()
+                rank = (my_rank + step) % camp
+                m_copy(update, half, my_base + rank, rank).wait_recv()
                 return carry
 
-            lax.fori_loop(1, devices, m_arrived, 0)
-            stage[half * half_channels : (half + 1) * half_channels] = (
-                mrecv[update, half].astype(F32).reshape(half_channels, local_rows, cols)
+            lax.fori_loop(1, camp, m_arrived, 0)
+            mixed = mrecv[update, half, :camp].astype(F32)
+            if update == 1:
+
+                def m_far_arrived(step, carry):
+                    rank = (my_rank + step) % camp
+                    m_copy(update, half, far_base + rank, camp + rank).wait_recv()
+                    return carry
+
+                lax.fori_loop(0, camp, m_far_arrived, 0)
+                mixed = mixed + mrecv[update, half, camp:].astype(F32)
+            stage[half * half_channels : (half + 1) * half_channels] = mixed.reshape(
+                half_channels, local_rows, cols
             )
 
         normalise(stage, 2 * update + 1)
@@ -362,21 +409,34 @@
         else:
             out[...] = fresh
 
-    def sent(step, carry):
-        device = (me + step) % devices
-        for update in range(2):
-            for half in range(2):
-                lr_copy(update, half, device, me).wait_send()
-                m_copy(update, half, device, me).wait_send()
-        return carry
-
-    lax.fori_loop(1, devices, sent, 0)
+    for update in range(2):
+        for half in range(2):
+
+            def near_sent(step, carry):
+                device = my_base + (my_rank + step) % camp
+                l_copy(update, half, device, my_rank).wait_send()
+                r_copy(update, half, device, my_rank).wait_send()
+                m_copy(update, half, device, my_rank).wait_send()
+                return carry
+
+            lax.fori_loop(1, camp, near_sent, 0)
+
+            def far_sent(step, carry):
+                device = far_base + (my_rank + step) % camp
+                if update == 0:
+                    r_copy(update, half, device, me).wait_send()
+                else:
+                    m_copy(update, half, device, camp + my_rank).wait_send()
+                return carry
+
+            lax.fori_loop(0, camp, far_sent, 0)
 
 
 def fused_body(rows_count, halves, pair, mask, gain_in, w_proj, w_gate, gain_out, w_out):
     channels, local_rows, cols = pair.shape
     devices = rows_count * halves
-    own = channels // devices // 2
+    camp = devices // 2
+    own = channels // camp // 2
     slab = own * local_rows
     pack = own * 4
     wide = local_rows * cols
@@ -392,7 +452,7 @@
         + [
             pltpu.VMEM(pair.shape, F32),
             pltpu.VMEM(pair.shape, F32),
-            pltpu.VMEM((2, devices // 2, 4 * pack, channels), BF16),
+            pltpu.VMEM((2, camp // 2, 4 * pack, channels), BF16),
             pltpu.VMEM((2, channels, channels), BF16),
             pltpu.VMEM((2, channels, channels), BF16),
             pltpu.VMEM((4, channels, cols), F32),
@@ -400,11 +460,15 @@
             pltpu.VMEM((channels, wide), F32),
             pltpu.VMEM((8, wide), F32),
             pltpu.VMEM((2, pack, local_rows, cols), F32),
-            pltpu.VMEM((2, 2, devices, 2, slab, cols), BF16),
-            pltpu.VMEM((2, 2, devices, 2, slab, cols), BF16),
+            pltpu.VMEM((2, 2, camp, slab, cols), BF16),
+            pltpu.VMEM((2, 2, camp, slab, cols), BF16),
+            pltpu.VMEM((2, 2, camp, slab, cols), BF16),
+            pltpu.VMEM((2, 2, devices, slab, cols), BF16),
             pltpu.VMEM((2, 2, devices, slab, cols), BF16),
             pltpu.VMEM((2, 2, devices, slab, cols), BF16),
             pltpu.SemaphoreType.DMA((7,)),
+            pltpu.SemaphoreType.DMA((2, 2, camp)),
+            pltpu.SemaphoreType.DMA((2, 2, camp)),
             pltpu.SemaphoreType.DMA((2, 2, devices)),
             pltpu.SemaphoreType.DMA((2, 2, devices)),
             pltpu.SemaphoreType.DMA((2, 2, devices)),
@@ -424,7 +488,7 @@
     fits = (
         lax.axis_size("ch") == 1
         and hidden == channels
-        and devices % 4 == 0
+        and devices % 8 == 0
         and local_rows == 8
         and cols == devices * local_rows
         and channels == devices * 8

time: 53.6 us -> 52.9 us (0.987)
  Pallas kernels: 51.8 us -> 51 us
    pallas_call x1, Pallas kernels: 51.8 us -> 51 us  [fused_body(): pl.pallas_call(functools.partial(kernel, rows_count, halves), out_shape=j...]
where the time goes in v3:
time: 52.9 us; the launch traced here: 52.7 us
  Pallas kernels  51 us (96%)
  local copies, waits for them, and re-layouts  1.67 us (3%)
    pallas_call x1, Pallas kernels, fused_body(): pl.pallas_call(functools.partial(kernel, rows_count, halves), out_shape=j...  51 us
    unnamed x1, local copies, waits for them, and re-layouts  1.67 us

profile of v3, /device:TPU:0, one launch (start us, length us, event | category | flops | bytes accessed | tf_op | source)
XLA Modules:
  0.0 52.7 jit_solution(3716813392603017089)
XLA Ops:
  0.0 51.0 %shard_map.73 = bf16[128,8,128]{2,1,0:T(8,128)(2,1)} custom-call(bf16[128,8,128]{2,1,0:T(8,128)(2,1)} %pair_hbm.1, s32[1,128]{1,0:T(1,128)} %bitcast.1, f32[2,128]{1,0:T(2,128)} %gain_in_hbm.1, bf16[2,128,512]{2,1,0:T(8,128)(2,1)} %w_proj_hbm.1, bf16[2,128,128]{2,1,0:T(8,128)(2,1)} %w_gate_hbm.1, f32[2,128]{1,0:T(2,128)} %gain_out_hbm.1, ...), custom_call_target="tpu_custom_call" | custom-call | tf_op jit(solution)/shard_map/pallas_call | solution.py:446
  51.1 1.7 %copy.9 = bf16[128,8,128]{2,1,0:T(8,128)(2,1)} copy(bf16[128,8,128]{2,1,0:T(8,128)(2,1)} %shard_map.73) | data formatting | bytes 524288

commit v4 on v3

--- a/solution.py
+++ b/solution.py
@@ -291,9 +291,18 @@
                     rank = group * plane + (my_seat + seat) % plane
                     if update == 0:
                         r_copy(update, half, far_base + rank, r_slot).start()
-                    if step < planes or seat > 0:
+                    if update == 1 and (step < planes or seat > 0):
                         l_copy(update, half, my_base + rank, my_rank).start()
                         r_copy(update, half, my_base + rank, r_slot).start()
+            if update == 0:
+
+                def near_step(step, carry):
+                    rank = (my_rank + step) % camp
+                    r_copy(update, half, my_base + rank, r_slot).start()
+                    l_copy(update, half, my_base + rank, my_rank).start()
+                    return carry
+
+                lax.fori_loop(1, camp, near_step, 0)
             lrecv[update, half, my_rank] = lsend[update, half, my_rank]
             rrecv[update, half, r_slot] = rsend[update, half, my_rank]
 

time: 52.9 us -> 52.1 us (0.985)
  Pallas kernels: 51 us -> 50.2 us
    pallas_call x1, Pallas kernels: 51 us -> 50.2 us  [fused_body(): pl.pallas_call(functools.partial(kernel, rows_count, halves), out_shape=j...]
where the time goes in v4:
time: 52.1 us; the launch traced here: 51.9 us
  Pallas kernels  50.2 us (96%)
  local copies, waits for them, and re-layouts  1.67 us (3%)
    pallas_call x1, Pallas kernels, fused_body(): pl.pallas_call(functools.partial(kernel, rows_count, halves), out_shape=j...  50.2 us
    unnamed x1, local copies, waits for them, and re-layouts  1.67 us

profile of v4, /device:TPU:0, one launch (start us, length us, event | category | flops | bytes accessed | tf_op | source)
XLA Modules:
  0.0 51.9 jit_solution(4418267289596733172)
XLA Ops:
  0.0 50.2 %shard_map.73 = bf16[128,8,128]{2,1,0:T(8,128)(2,1)} custom-call(bf16[128,8,128]{2,1,0:T(8,128)(2,1)} %pair_hbm.1, s32[1,128]{1,0:T(1,128)} %bitcast.1, f32[2,128]{1,0:T(2,128)} %gain_in_hbm.1, bf16[2,128,512]{2,1,0:T(8,128)(2,1)} %w_proj_hbm.1, bf16[2,128,128]{2,1,0:T(8,128)(2,1)} %w_gate_hbm.1, f32[2,128]{1,0:T(2,128)} %gain_out_hbm.1, ...), custom_call_target="tpu_custom_call" | custom-call | tf_op jit(solution)/shard_map/pallas_call | solution.py:455
  50.2 1.7 %copy.9 = bf16[128,8,128]{2,1,0:T(8,128)(2,1)} copy(bf16[128,8,128]{2,1,0:T(8,128)(2,1)} %shard_map.73) | data formatting | bytes 524288
